TPU v7x, 256 devices: a whole 4x4x8 slice. The times are simulated.
256 devices in a mesh: row: 8 (over x, y_lo), col: 32 (over z, y_hi, core).
Axes of the slice: x: 4, y: 4 (y_hi: 2, y_lo: 2; y = y_hi * 2 + y_lo), z: 8, core: 2. Of those that a mesh axis runs over, the one named last changes fastest.
Arguments:
- queries: bfloat16 [1024, 2560], P(('row', 'col')), may hold values from -4 to 4
- passages: bfloat16 [1024, 2560], P(('row', 'col')), may hold values from -1 to 1
- positive: int32 [1024], P(('row', 'col')), may hold values from 0 to 1023, each once
Outputs:
- loss: float32 [], replicated
- grad_queries: bfloat16 [1024, 2560], P(('row', 'col'))
- grad_passages: bfloat16 [1024, 2560], P(('row', 'col'))
Inputs may be any that keep to these rules, and one draw needn't show every extreme that they name: Each passage is the positive of exactly one query.
All inputs are finite; a program needn't handle non-finite values.
Results may differ from a plain program's by a relative error of at most 0.0045.
Values may be sent and summed in bfloat16 or wider, within the bound.
A program may use at most 64 MiB of HBM per device.

v0:
```python
import jax
import jax.numpy as jnp
from jax import lax
from jax.sharding import PartitionSpec as P


def per_device(queries, passages, positive):
    own_rows = queries.shape[0]
    query_block, target_block = (
        lax.all_gather(queries, "col", axis=0, tiled=True),
        lax.all_gather(positive, "col", axis=0, tiled=True),
    )
    passage_block = lax.all_gather(passages, "row", axis=0, tiled=True)
    col_count = lax.axis_size("col")
    row_count = lax.axis_size("row")
    col_index = lax.axis_index("col")
    slots = jnp.arange(passage_block.shape[0], dtype=jnp.int32)
    column_ids = (slots // own_rows * col_count + col_index) * own_rows + slots % own_rows
    scores = lax.dot_general(
        query_block, passage_block, (((1,), (1,)), ((), ())), preferred_element_type=jnp.float32
    )
    matched = target_block[:, None] == column_ids[None, :]
    local_peak = jnp.max(scores, axis=1)
    local_positive = jnp.sum(jnp.where(matched, scores, jnp.zeros_like(scores)), axis=1)
    row_peak = lax.pmax(local_peak, "col")
    powers = jnp.exp(scores - row_peak[:, None])
    totals, positive_score = lax.psum((jnp.sum(powers, axis=1), local_positive), "col")
    block_loss = jnp.sum(row_peak + jnp.log(totals) - positive_score)
    loss = lax.psum(block_loss, "row") / (query_block.shape[0] * row_count)
    weights = (powers / totals[:, None] - matched.astype(jnp.float32)).astype(jnp.bfloat16)
    picked = weights
    grad_query = lax.psum_scatter(
        jnp.dot(picked, passage_block, preferred_element_type=jnp.float32),
        "col",
        scatter_dimension=0,
        tiled=True,
    )
    picked = weights
    grad_pass = lax.psum_scatter(
        lax.dot_general(
            picked, query_block, (((0,), (0,)), ((), ())), preferred_element_type=jnp.float32
        ),
        "row",
        scatter_dimension=0,
        tiled=True,
    )
    return (loss, grad_query.astype(jnp.bfloat16), grad_pass.astype(jnp.bfloat16))


def solution(mesh):
    placed = (P(("row", "col"), None), P(("row", "col"), None), P(("row", "col")))
    return jax.shard_map(
        per_device,
        mesh=mesh,
        in_specs=placed,
        out_specs=(P(), P(("row", "col"), None), P(("row", "col"), None)),
        check_vma=False,
    )
```

profile of v0, /device:TPU:0, one launch (start us, length us, event | category | flops | bytes accessed | tf_op | source)
XLA Modules:
  0.0 413.2 jit_solution(14612436180394490417)
XLA Ops:
  0.7 1.3 dynamic-slice.3
  2.6 1.3 fusion.12
  5.2 0.9 dynamic-update-slice
  6.1 19.3 %all-reduce = s32[128]{0:T(128)S(1)} all-reduce(s32[128]{0:T(128)S(1)} %dynamic-update-slice), channel_id=1, replica_groups=mesh['row'=8,'col'=32] {'col'}, use_global_device_ids=true, to_apply=%add | all-reduce | flops 128 | bytes 1024
  25.4 28.5 %all-gather.1 = bf16[8,4,2560]{2,1,0:T(4,128)(2,1)S(1)} all-gather(bf16[1,4,2560]{2,1,0:T(4,128)(2,1)} %bitcast.9), channel_id=1, replica_groups=mesh['row'=8,'col'=32] {'row'}, dimensions={0}, use_global_device_ids=true | all-gather | bytes 184320 | tf_op jit(solution)/shard_map/all_gather | solution.py:13
  54.0 40.8 %all-gather = bf16[32,4,2560]{2,1,0:T(4,128)(2,1)S(1)} all-gather(bf16[1,4,2560]{2,1,0:T(4,128)(2,1)} %bitcast.10), channel_id=1, replica_groups=mesh['row'=8,'col'=32] {'col'}, dimensions={0}, use_global_device_ids=true | all-gather | bytes 675840 | tf_op jit(solution)/shard_map/all_gather | solution.py:10
  94.7 0.1 reshape.37
  94.9 0.3 fusion.13
  95.2 66.1 %pmax.7 = f32[128]{0:T(128)S(1)} all-reduce(f32[128]{0:T(128)S(1)} %get-tuple-element.11), channel_id=1, replica_groups=mesh['row'=8,'col'=32] {'col'}, use_global_device_ids=true, to_apply=%region_1.2 | all-reduce | flops 128 | bytes 1024 | tf_op jit(solution)/shard_map/pmax | solution.py:25
  161.3 0.1 fusion.3
  161.4 65.0 %psum.21 = f32[128]{0:T(128)S(1)} all-reduce(f32[128]{0:T(128)S(1)} %get-tuple-element.3), channel_id=1, replica_groups=mesh['row'=8,'col'=32] {'col'}, use_global_device_ids=true, to_apply=%region_3.4 | all-reduce | flops 128 | bytes 1024 | tf_op jit(solution)/shard_map/psum | solution.py:27
  226.4 0.3 fusion.8
  226.7 0.4 fusion.10
  227.1 144.4 %all-reduce.7 = (f32[128]{0:T(128)S(1)}, bf16[128,2560]{1,0:T(8,128)(2,1)S(1)}) all-reduce(f32[128]{0:T(128)S(1)} %get-tuple-element.4, f32[128,2560]{1,0:T(8,128)S(1)} %fusion.10), channel_id=1, replica_groups=mesh['row'=8,'col'=32] {'col'}, use_global_device_ids=true, to_apply=%region_5.6 | all-reduce | flops 327808 | bytes 1967104 | tf_op jit(solution)/shard_map/psum | solution.py:27
  371.5 0.6 subtract_reduce_fusion
  372.1 38.0 %all-reduce.8 = (f32[]{:T(128)}, bf16[32,2560]{1,0:T(8,128)(2,1)S(1)}) all-reduce(f32[]{:T(128)} %subtract_reduce_fusion, f32[32,2560]{1,0:T(8,128)S(1)} %fusion.8), channel_id=1, replica_groups=mesh['row'=8,'col'=32] {'row'}, use_global_device_ids=true, to_apply=%region_7.8 | all-reduce | flops 81921 | bytes 491528 | tf_op jit(solution)/shard_map/psum | solution.py:29
  410.8 0.6 dynamic-slice_convert_fusion
  411.4 0.6 dynamic-slice_convert_fusion.1
  (3 shorter events, 0.1 us)
where the time goes:
time: 413 us
  blocking collectives  402 us (97%)
  local copies, waits for them, and re-layouts  4.91 us (1%)
  between operations  4.43 us (1%)
    psum x2, blocking collectives, per_device(): lax.psum((jnp.sum(powers, axis=1), local_positive), 'col')  209 us
    pmax x1, blocking collectives, per_device(): row_peak = lax.pmax(local_peak, 'col')  66.1 us
    all_gather x1, blocking collectives, per_device(): lax.all_gather(queries, 'col', axis=0, tiled=True)  40.8 us
    psum x1, blocking collectives, per_device(): loss = lax.psum(block_loss, 'row') / (query_block.shape[0] * row_count)  38 us
    all_gather x1, blocking collectives, per_device(): passage_block = lax.all_gather(passages, 'row', axis=0, tiled=True)  28.5 us
    unnamed x1, blocking collectives  19.3 us

commit v1 on v0

v1 whole, which is shorter than its diff:
```python
import functools

import jax
import jax.numpy as jnp
from jax import lax
from jax.experimental import pallas as pl
from jax.experimental.pallas import tpu as pltpu
from jax.sharding import PartitionSpec as P

MESH = pl.DeviceIdType.MESH
X, Y, Z, CORES = 4, 4, 8, 2
PLANE = X * Y
LANES = 128
F32, BF16 = jnp.float32, jnp.bfloat16


def device_of(x, y, z, core):
    return (x * 2 + y % 2, z * 4 + (y // 2) * 2 + core)


def kernel(total, q_ref, p_ref, pos_ref, loss_ref, gq_ref, gp_ref,
           stage, qbuf, pbuf, qwide, pwide, half_own, half_other, statbuf, stat_own,
           gq_send, gq_recv, gp_send, gp_recv, lossbuf, loss_own,
           local_sem, send_sem, recv_sem):
    row, col = lax.axis_index("row"), lax.axis_index("col")
    x, z, core = row // 2, col // 4, col % 2
    y = ((col // 2) % 2) * 2 + row % 2
    chip = x * Y + y
    own = q_ref.shape[0]
    half = q_ref.shape[1] // CORES
    q_slot, p_slot = chip * CORES + core, z * CORES + core
    other = device_of(x, y, z, 1 - core)

    def plane_peer(step):
        to = (chip + step) % PLANE
        return to, to // Y, to % Y

    barrier = pltpu.get_barrier_semaphore()

    def greet_plane(step, _):
        _, px, py = plane_peer(step)
        for c in range(CORES):
            pl.semaphore_signal(barrier, inc=1, device_id=device_of(px, py, z, c), device_id_type=MESH)
        return _

    def greet_line(step, _):
        for c in range(CORES):
            pl.semaphore_signal(barrier, inc=1, device_id=device_of(x, y, (z + step) % Z, c), device_id_type=MESH)
        return _

    pl.semaphore_signal(barrier, inc=1, device_id=other, device_id_type=MESH)
    lax.fori_loop(1, PLANE, greet_plane, 0)
    lax.fori_loop(1, Z, greet_line, 0)

    lane = lax.broadcasted_iota(jnp.int32, (1, LANES), 1)
    for h in range(CORES):
        stage[h, :, :half] = q_ref[:, h * half:(h + 1) * half]
    codes = []
    for k in range(own):
        index = pos_ref[k]
        codes.append(((lane == index // 32) | (lane == 32 + index % 32)).astype(F32))
    code = jnp.concatenate(codes, axis=0).astype(BF16)
    for h in range(CORES):
        stage[h, :, half:] = code

    pl.semaphore_wait(barrier, PLANE * CORES + (Z - 1) * CORES - 1)

    def send(src, dst, to, kind):
        return pltpu.make_async_remote_copy(
            src_ref=src, dst_ref=dst, send_sem=send_sem.at[kind], recv_sem=recv_sem.at[kind],
            device_id=to, device_id_type=MESH)

    def p_half(h):
        return p_ref.at[:, pl.ds(pl.multiple_of(h * half, LANES), half)]

    def gather_plane(step, _):
        _, px, py = plane_peer(step)
        for c in range(CORES):
            send(stage.at[c], qbuf.at[q_slot], device_of(px, py, z, c), 0).start()
        return _

    def gather_line(step, _):
        for c in range(CORES):
            send(p_half(c), pbuf.at[p_slot], device_of(x, y, (z + step) % Z, c), 1).start()
        return _

    lax.fori_loop(1, Z, gather_line, 0)
    lax.fori_loop(1, PLANE, gather_plane, 0)
    send(stage.at[1 - core], qbuf.at[q_slot], other, 0).start()
    send(p_half(1 - core), pbuf.at[p_slot], other, 1).start()
    own_q = pltpu.make_async_copy(stage.at[core], qbuf.at[q_slot], local_sem.at[0])
    own_p = pltpu.make_async_copy(p_half(core), pbuf.at[p_slot], local_sem.at[1])
    own_q.start()
    own_p.start()
    own_q.wait()
    own_p.wait()

    def wait_recv(ref, kind):
        pltpu.make_async_copy(ref, ref, recv_sem.at[kind]).wait()

    def wait_send(ref, kind):
        pltpu.make_async_copy(ref, ref, send_sem.at[kind]).wait()

    p_count, q_count = Z * CORES, PLANE * CORES
    wait_recv(pbuf.at[pl.ds(0, p_count - 1)], 1)
    for s in range(p_count):
        pwide[s * own:(s + 1) * own, :] = pbuf[s].astype(F32)
    passages = pwide[...].astype(BF16)
    wait_recv(qbuf.at[pl.ds(0, q_count - 1)], 0)
    for s in range(q_count):
        qwide[s * own:(s + 1) * own, :] = qbuf[s].astype(F32)
    queries = qwide[:, :half].astype(BF16)
    q_code = qwide[:, half:].astype(BF16)

    contract_last = (((1,), (1,)), ((), ()))
    half_own[...] = lax.dot_general(passages, queries, contract_last, preferred_element_type=F32)
    trade = send(half_own, half_other, other, 2)
    trade.start()
    n_p = p_count * own
    slot = lax.broadcasted_iota(jnp.int32, (n_p, LANES), 0)
    zz, cc, kk = slot // (CORES * own), (slot // own) % CORES, slot % own
    p_row, p_col = device_of(x, y, zz, cc)
    p_id = (p_row * 32 + p_col) * own + kk
    p_lane = lax.broadcasted_iota(jnp.int32, (n_p, LANES), 1)
    p_code = ((p_lane == p_id // 32) | (p_lane == 32 + p_id % 32)).astype(F32).astype(BF16)
    matched = lax.dot_general(p_code, q_code, contract_last, preferred_element_type=F32) > 1.5
    trade.wait()
    scores = half_own[...] + half_other[...]

    peak = jnp.max(scores, axis=0, keepdims=True)
    summed = jnp.sum(jnp.exp(scores - peak), axis=0, keepdims=True)
    picked = jnp.sum(jnp.where(matched, scores, 0.0), axis=0, keepdims=True)
    stat_own[0:1, :] = peak
    stat_own[1:2, :] = summed
    stat_own[2:3, :] = picked
    stat_own[3:8, :] = jnp.zeros((5, stat_own.shape[1]), F32)
    statbuf[pl.ds(chip, 1)] = stat_own[...][None]

    def send_stat(step, _):
        _, px, py = plane_peer(step)
        send(stat_own, statbuf.at[chip], device_of(px, py, z, core), 3).start()
        return _

    lax.fori_loop(1, PLANE, send_stat, 0)
    wait_recv(statbuf.at[pl.ds(0, PLANE - 1)], 3)
    stats = statbuf[...]
    peaks, sums, picks = stats[:, 0:1], stats[:, 1:2], stats[:, 2:3]
    row_peak = jnp.max(peaks, axis=0)
    totals = jnp.sum(sums * jnp.exp(peaks - row_peak[None]), axis=0)
    positive_score = jnp.sum(picks, axis=0)
    weights = (jnp.exp(scores - row_peak) / totals - matched.astype(F32)).astype(BF16)

    for at in range(0, half, 256):
        part = lax.dot_general(weights, passages[:, at:at + 256], (((0,), (0,)), ((), ())),
                               preferred_element_type=F32).astype(BF16)
        for s in range(q_count):
            gq_send[s, :, at:at + 256] = part[s * own:(s + 1) * own]

    def give_plane(step, _):
        to, px, py = plane_peer(step)
        for c in range(CORES):
            send(gq_send.at[to * CORES + c], gq_recv.at[chip, core], device_of(px, py, z, c), 4).start()
        return _

    lax.fori_loop(1, PLANE, give_plane, 0)
    send(gq_send.at[chip * CORES + 1 - core], gq_recv.at[chip, core], other, 4).start()
    own_gq = pltpu.make_async_copy(gq_send.at[q_slot], gq_recv.at[chip, core], local_sem.at[2])
    own_gq.start()
    for at in range(0, half, 256):
        part = jnp.dot(weights, queries[:, at:at + 256], preferred_element_type=F32).astype(BF16)
        for s in range(p_count):
            gp_send[s, :, at:at + 256] = part[s * own:(s + 1) * own]

    def give_line(step, _):
        to = (z + step) % Z
        for c in range(CORES):
            send(gp_send.at[to * CORES + c], gp_recv.at[z, core], device_of(x, y, to, c), 5).start()
        return _

    lax.fori_loop(1, Z, give_line, 0)
    send(gp_send.at[z * CORES + 1 - core], gp_recv.at[z, core], other, 5).start()
    own_gp = pltpu.make_async_copy(gp_send.at[p_slot], gp_recv.at[z, core], local_sem.at[3])
    own_gp.start()

    block_loss = row_peak + jnp.log(totals) - positive_score
    loss_own[...] = jnp.broadcast_to(block_loss, loss_own.shape)
    lossbuf[pl.ds(z, 1)] = loss_own[...][None]

    def give_loss(step, _):
        send(loss_own, lossbuf.at[z], device_of(x, y, (z + step) % Z, core), 6).start()
        return _

    lax.fori_loop(1, Z, give_loss, 0)
    wait_recv(lossbuf.at[pl.ds(0, Z - 1)], 6)
    loss_ref[0, 0] = jnp.sum(jnp.sum(lossbuf[...], axis=0)[0:1]) / total

    own_gp.wait()
    wait_recv(gp_send.at[pl.ds(0, p_count - 1)], 5)
    for h in range(CORES):
        acc = gp_recv[0, h].astype(F32)
        for k in range(1, Z):
            acc += gp_recv[k, h].astype(F32)
        gp_ref[:, h * half:(h + 1) * half] = acc.astype(BF16)
    own_gq.wait()
    wait_recv(gq_send.at[pl.ds(0, q_count - 1)], 4)
    for h in range(CORES):
        acc = gq_recv[0, h].astype(F32)
        for k in range(1, PLANE):
            acc += gq_recv[k, h].astype(F32)
        gq_ref[:, h * half:(h + 1) * half] = acc.astype(BF16)

    wait_send(qbuf.at[pl.ds(0, q_count - 1)], 0)
    wait_send(pbuf.at[pl.ds(0, p_count - 1)], 1)
    wait_send(statbuf.at[pl.ds(0, PLANE - 1)], 3)
    wait_send(gq_send.at[pl.ds(0, q_count - 1)], 4)
    wait_send(gp_send.at[pl.ds(0, p_count - 1)], 5)
    wait_send(lossbuf.at[pl.ds(0, Z - 1)], 6)


def per_device(queries, passages, positive):
    own, width = queries.shape
    half = width // CORES
    n_q, n_p = PLANE * CORES, Z * CORES
    vmem = pl.BlockSpec(memory_space=pltpu.VMEM)
    loss, gq, gp = pl.pallas_call(
        functools.partial(kernel, n_q * own * Z),
        out_shape=(
            jax.ShapeDtypeStruct((1, 1), F32),
            jax.ShapeDtypeStruct((own, width), BF16),
            jax.ShapeDtypeStruct((own, width), BF16),
        ),
        in_specs=[vmem, vmem, pl.BlockSpec(memory_space=pltpu.SMEM)],
        out_specs=(pl.BlockSpec(memory_space=pltpu.SMEM), vmem, vmem),
        scratch_shapes=[
            pltpu.VMEM((CORES, own, half + LANES), BF16),
            pltpu.VMEM((n_q, own, half + LANES), BF16),
            pltpu.VMEM((n_p, own, half), BF16),
            pltpu.VMEM((n_q * own, half + LANES), F32),
            pltpu.VMEM((n_p * own, half), F32),
            pltpu.VMEM((n_p * own, n_q * own), F32),
            pltpu.VMEM((n_p * own, n_q * own), F32),
            pltpu.VMEM((PLANE, 8, n_q * own), F32),
            pltpu.VMEM((8, n_q * own), F32),
            pltpu.VMEM((n_q, own, half), BF16),
            pltpu.VMEM((PLANE, CORES, own, half), BF16),
            pltpu.VMEM((n_p, own, half), BF16),
            pltpu.VMEM((Z, CORES, own, half), BF16),
            pltpu.VMEM((Z, 8, n_q * own), F32),
            pltpu.VMEM((8, n_q * own), F32),
            pltpu.SemaphoreType.DMA((4,)),
            pltpu.SemaphoreType.DMA((7,)),
            pltpu.SemaphoreType.DMA((7,)),
        ],
        compiler_params=pltpu.CompilerParams(
            collective_id=0, has_side_effects=True, vmem_limit_bytes=32 * 1024 * 1024),
    )(queries, passages, positive)
    return loss[0, 0], gq, gp


def solution(mesh):
    placed = (P(("row", "col"), None), P(("row", "col"), None), P(("row", "col")))
    return jax.shard_map(
        per_device,
        mesh=mesh,
        in_specs=placed,
        out_specs=(P(), P(("row", "col"), None), P(("row", "col"), None)),
        check_vma=False,
    )
```

time: 413 us -> 40.5 us (0.10)
  the two profiles are of different devices: /device:TPU:0 before, /device:TPU:1 now
where the time goes in v1:
time: 40.5 us; the launch traced here: 40.3 us
  Pallas kernels  34.6 us (85%)
  local copies, waits for them, and re-layouts  3.32 us (8%)
  between operations  2.38 us (6%)
    pallas_call x1, Pallas kernels, per_device(): pl.pallas_call(functools.partial(kernel, n_q * own * Z), out_shape=(jax.S...  34.6 us
    unnamed x8, local copies, waits for them, and re-layouts  3.32 us

profile of v1, /device:TPU:1, one launch (start us, length us, event | category | flops | bytes accessed | tf_op | source)
XLA Modules:
  0.0 40.3 jit_solution(2994227025222080476)
XLA Ops:
  0.6 0.0 copy-start
  0.6 0.7 %copy-done = bf16[4,2560]{1,0:T(4,128)(2,1)S(1)} copy-done((bf16[4,2560]{1,0:T(4,128)(2,1)S(1)}, bf16[4,2560]{1,0:T(4,128)(2,1)}, u32[]{:S(2)}) %copy-start) | copy-done | bytes 20504
  1.4 0.0 copy-start.1
  1.4 0.7 %copy-done.1 = bf16[4,2560]{1,0:T(4,128)(2,1)S(1)} copy-done((bf16[4,2560]{1,0:T(4,128)(2,1)S(1)}, bf16[4,2560]{1,0:T(4,128)(2,1)}, u32[]{:S(2)}) %copy-start.1) | copy-done | bytes 20504
  2.1 0.0 copy-start.2
  2.1 0.7 %copy-done.2 = s32[4]{0:T(128)S(1)} copy-done((s32[4]{0:T(128)S(1)}, s32[4]{0:T(128)}, u32[]{:S(2)}) %copy-start.2) | copy-done | bytes 40
  2.7 34.6 %shard_map.58 = (f32[1,1]{1,0:T(1,128)}, bf16[4,2560]{1,0:T(4,128)(2,1)S(1)}, bf16[4,2560]{1,0:T(4,128)(2,1)S(1)}) custom-call(bf16[4,2560]{1,0:T(4,128)(2,1)S(1)} %copy-done, bf16[4,2560]{1,0:T(4,128)(2,1)S(1)} %copy-done.1, s32[4]{0:T(128)S(1)} %copy-done.2), custom_call_target="tpu_custom_call" | custom-call | tf_op jit(solution)/shard_map/pallas_call | solution.py:225
  37.9 0.6 %copy.10 = bf16[4,2560]{1,0:T(4,128)(2,1)} copy(bf16[4,2560]{1,0:T(4,128)(2,1)S(1)} %get-tuple-element.13) | data formatting | bytes 40960
  38.6 0.6 %copy.11 = bf16[4,2560]{1,0:T(4,128)(2,1)} copy(bf16[4,2560]{1,0:T(4,128)(2,1)S(1)} %get-tuple-element.14) | data formatting | bytes 40960
Async XLA Ops:
  0.6 0.7 %copy-start = (bf16[4,2560]{1,0:T(4,128)(2,1)S(1)}, bf16[4,2560]{1,0:T(4,128)(2,1)}, u32[]{:S(2)}) copy-start(bf16[4,2560]{1,0:T(4,128)(2,1)} %q_ref.1) | copy-start | bytes 61444
  1.4 0.7 %copy-start.1 = (bf16[4,2560]{1,0:T(4,128)(2,1)S(1)}, bf16[4,2560]{1,0:T(4,128)(2,1)}, u32[]{:S(2)}) copy-start(bf16[4,2560]{1,0:T(4,128)(2,1)} %p_ref.1) | copy-start | bytes 61444
  2.1 0.7 %copy-start.2 = (s32[4]{0:T(128)S(1)}, s32[4]{0:T(128)}, u32[]{:S(2)}) copy-start(s32[4]{0:T(128)} %pos_ref.1) | copy-start | bytes 52

commit v2 on v1

v2 whole, which is shorter than its diff:
```python
import functools

import jax
import jax.numpy as jnp
from jax import lax
from jax.experimental import pallas as pl
from jax.experimental.pallas import tpu as pltpu
from jax.sharding import PartitionSpec as P

MESH = pl.DeviceIdType.MESH
X, Y, Z, CORES = 4, 4, 8, 2
PLANE = X * Y
LANES = 128
F32, BF16 = jnp.float32, jnp.bfloat16


def ring(step, n):
    return min(step, n - step)


PLANE_STEPS = sorted(
    ((dx, dy) for dx in range(X) for dy in range(Y) if dx or dy),
    key=lambda s: -(ring(s[0], X) + ring(s[1], Y)))
LINE_STEPS = sorted(range(1, Z), key=lambda s: -ring(s, Z))


def device_of(x, y, z, core):
    return (x * 2 + y % 2, z * 4 + (y // 2) * 2 + core)


def kernel(total, q_hbm, p_hbm, pos_hbm, loss_ref, g_ref,
           pos, stage, p_own, qbuf, pbuf, qwide, pwide, half_own, half_other, statbuf, stat_own,
           gq_send, gq_recv, gp_send, gp_recv, lossbuf, loss_own,
           local_sem, send_sem, recv_sem):
    row, col = lax.axis_index("row"), lax.axis_index("col")
    x, z, core = row // 2, col // 4, col % 2
    y = ((col // 2) % 2) * 2 + row % 2
    chip = x * Y + y
    own = q_hbm.shape[0]
    half = q_hbm.shape[1] // CORES
    p_count, q_count = Z * CORES, PLANE * CORES
    q_slot, p_slot = chip * CORES + core, z * CORES + core
    other = device_of(x, y, z, 1 - core)
    plane = [((x + dx) % X, (y + dy) % Y) for dx, dy in PLANE_STEPS]
    line = [(z + dz) % Z for dz in LINE_STEPS]

    barrier = pltpu.get_barrier_semaphore()

    def greet(device):
        pl.semaphore_signal(barrier, inc=1, device_id=device, device_id_type=MESH)

    for pz in line:
        for c in range(CORES):
            greet(device_of(x, y, pz, c))
    for px, py in plane:
        for c in range(CORES):
            greet(device_of(px, py, z, c))
    greet(other)

    loads = [pltpu.make_async_copy(pos_hbm, pos, local_sem.at[4])]
    for h in range(CORES):
        part = pl.ds(h * half, half)
        loads.append(pltpu.make_async_copy(p_hbm.at[:, part], p_own.at[h], local_sem.at[5 + h]))
        loads.append(pltpu.make_async_copy(q_hbm.at[:, part], stage.at[h, :, pl.ds(0, half)], local_sem.at[7 + h]))
    for load in loads:
        load.start()
    loads[0].wait()
    lane = lax.broadcasted_iota(jnp.int32, (1, LANES), 1)
    codes = []
    for k in range(own):
        index = pos[k]
        codes.append(((lane == index // 32) | (lane == 32 + index % 32)).astype(F32))
    code = jnp.concatenate(codes, axis=0).astype(BF16)
    for load in loads[1:]:
        load.wait()
    for h in range(CORES):
        stage[h, :, half:] = code

    pl.semaphore_wait(barrier, (PLANE + Z - 1) * CORES - 1)

    def send(src, dst, to, kind):
        return pltpu.make_async_remote_copy(
            src_ref=src, dst_ref=dst, send_sem=send_sem.at[kind], recv_sem=recv_sem.at[kind],
            device_id=to, device_id_type=MESH)

    def gather_plane(px, py):
        for c in range(CORES):
            send(stage.at[c], qbuf.at[q_slot], device_of(px, py, z, c), 0).start()

    def gather_line(pz):
        for c in range(CORES):
            send(p_own.at[c], pbuf.at[p_slot], device_of(x, y, pz, c), 1).start()

    for k in range(PLANE - 1):
        gather_plane(*plane[k])
        if k % 2 == 0 and k // 2 < Z - 1:
            gather_line(line[k // 2])
    send(stage.at[1 - core], qbuf.at[q_slot], other, 0).start()
    send(p_own.at[1 - core], pbuf.at[p_slot], other, 1).start()
    own_q = pltpu.make_async_copy(stage.at[core], qbuf.at[q_slot], local_sem.at[0])
    own_p = pltpu.make_async_copy(p_own.at[core], pbuf.at[p_slot], local_sem.at[1])
    own_q.start()
    own_p.start()

    def wait_recv(ref, kind):
        pltpu.make_async_copy(ref, ref, recv_sem.at[kind]).wait()

    def wait_send(ref, kind):
        pltpu.make_async_copy(ref, ref, send_sem.at[kind]).wait()

    n_p = p_count * own
    slot = lax.broadcasted_iota(jnp.int32, (n_p, LANES), 0)
    p_row, p_col = device_of(x, y, slot // (CORES * own), (slot // own) % CORES)
    p_id = (p_row * 32 + p_col) * own + slot % own
    p_lane = lax.broadcasted_iota(jnp.int32, (n_p, LANES), 1)
    p_code = ((p_lane == p_id // 32) | (p_lane == 32 + p_id % 32)).astype(F32).astype(BF16)

    own_p.wait()
    own_q.wait()
    wait_recv(pbuf.at[pl.ds(0, p_count - 1)], 1)
    for s in range(p_count):
        pwide[s * own:(s + 1) * own, :] = pbuf[s].astype(F32)
    passages = pwide[...].astype(BF16)
    wait_recv(qbuf.at[pl.ds(0, q_count - 1)], 0)
    for s in range(q_count):
        qwide[s * own:(s + 1) * own, :] = qbuf[s].astype(F32)
    queries = qwide[:, :half].astype(BF16)
    q_code = qwide[:, half:].astype(BF16)

    contract_last = (((1,), (1,)), ((), ()))
    half_own[...] = lax.dot_general(passages, queries, contract_last, preferred_element_type=F32)
    trade = send(half_own, half_other, other, 2)
    trade.start()
    matched = lax.dot_general(p_code, q_code, contract_last, preferred_element_type=F32) > 1.5
    trade.wait()
    scores = half_own[...] + half_other[...]

    n_q = q_count * own
    peak = jnp.max(scores, axis=0, keepdims=True)
    stat_own[:, :n_q] = peak
    stat_own[:, n_q:2 * n_q] = jnp.sum(jnp.exp(scores - peak), axis=0, keepdims=True)
    stat_own[:, 2 * n_q:] = jnp.sum(jnp.where(matched, scores, 0.0), axis=0, keepdims=True)
    statbuf[pl.ds(chip, 1)] = stat_own[...][None]
    for px, py in plane:
        send(stat_own, statbuf.at[chip], device_of(px, py, z, core), 3).start()
    wait_recv(statbuf.at[pl.ds(0, PLANE - 1)], 3)
    stats = statbuf[...]
    peaks, sums, picks = stats[:, :, :n_q], stats[:, :, n_q:2 * n_q], stats[:, :, 2 * n_q:]
    row_peak = jnp.max(peaks, axis=0)
    totals = jnp.sum(sums * jnp.exp(peaks - row_peak[None]), axis=0)
    positive_score = jnp.sum(picks, axis=0)
    weights = (jnp.exp(scores - row_peak) / totals - matched.astype(F32)).astype(BF16)

    loss_own[...] = row_peak + jnp.log(totals) - positive_score
    lossbuf[pl.ds(z, 1)] = loss_own[...][None]
    for pz in line:
        send(loss_own, lossbuf.at[z], device_of(x, y, pz, core), 6).start()

    for at in range(0, half, 256):
        part = lax.dot_general(weights, passages[:, at:at + 256], (((0,), (0,)), ((), ())),
                               preferred_element_type=F32).astype(BF16)
        for s in range(q_count):
            gq_send[s, :, at:at + 256] = part[s * own:(s + 1) * own]
    for px, py in plane:
        for c in range(CORES):
            send(gq_send.at[(px * Y + py) * CORES + c], gq_recv.at[chip, core], device_of(px, py, z, c), 4).start()
    send(gq_send.at[chip * CORES + 1 - core], gq_recv.at[chip, core], other, 4).start()
    own_gq = pltpu.make_async_copy(gq_send.at[q_slot], gq_recv.at[chip, core], local_sem.at[2])
    own_gq.start()
    for at in range(0, half, 256):
        part = jnp.dot(weights, queries[:, at:at + 256], preferred_element_type=F32).astype(BF16)
        for s in range(p_count):
            gp_send[s, :, at:at + 256] = part[s * own:(s + 1) * own]
    for pz in line:
        for c in range(CORES):
            send(gp_send.at[pz * CORES + c], gp_recv.at[z, core], device_of(x, y, pz, c), 5).start()
    send(gp_send.at[z * CORES + 1 - core], gp_recv.at[z, core], other, 5).start()
    own_gp = pltpu.make_async_copy(gp_send.at[p_slot], gp_recv.at[z, core], local_sem.at[3])
    own_gp.start()

    wait_recv(lossbuf.at[pl.ds(0, Z - 1)], 6)
    loss_ref[0, 0] = jnp.sum(jnp.sum(lossbuf[...], axis=0)) / total

    own_gq.wait()
    wait_recv(gq_send.at[pl.ds(0, q_count - 1)], 4)
    for h in range(CORES):
        acc = gq_recv[0, h].astype(F32)
        for k in range(1, PLANE):
            acc += gq_recv[k, h].astype(F32)
        g_ref[0, :, h * half:(h + 1) * half] = acc.astype(BF16)
    own_gp.wait()
    wait_recv(gp_send.at[pl.ds(0, p_count - 1)], 5)
    for h in range(CORES):
        acc = gp_recv[0, h].astype(F32)
        for k in range(1, Z):
            acc += gp_recv[k, h].astype(F32)
        g_ref[1, :, h * half:(h + 1) * half] = acc.astype(BF16)

    wait_send(qbuf.at[pl.ds(0, q_count - 1)], 0)
    wait_send(pbuf.at[pl.ds(0, p_count - 1)], 1)
    wait_send(statbuf.at[pl.ds(0, PLANE - 1)], 3)
    wait_send(gq_send.at[pl.ds(0, q_count - 1)], 4)
    wait_send(gp_send.at[pl.ds(0, p_count - 1)], 5)
    wait_send(lossbuf.at[pl.ds(0, Z - 1)], 6)


def per_device(queries, passages, positive):
    own, width = queries.shape
    half = width // CORES
    n_q, n_p = PLANE * CORES, Z * CORES
    vmem, hbm = pl.BlockSpec(memory_space=pltpu.VMEM), pl.BlockSpec(memory_space=pltpu.HBM)
    loss, grads = pl.pallas_call(
        functools.partial(kernel, n_q * own * Z),
        out_shape=(
            jax.ShapeDtypeStruct((1, 1), F32),
            jax.ShapeDtypeStruct((2, own, width), BF16),
        ),
        in_specs=[hbm, hbm, hbm],
        out_specs=(pl.BlockSpec(memory_space=pltpu.SMEM), vmem),
        scratch_shapes=[
            pltpu.SMEM((own,), jnp.int32),
            pltpu.VMEM((CORES, own, half + LANES), BF16),
            pltpu.VMEM((CORES, own, half), BF16),
            pltpu.VMEM((n_q, own, half + LANES), BF16),
            pltpu.VMEM((n_p, own, half), BF16),
            pltpu.VMEM((n_q * own, half + LANES), F32),
            pltpu.VMEM((n_p * own, half), F32),
            pltpu.VMEM((n_p * own, n_q * own), F32),
            pltpu.VMEM((n_p * own, n_q * own), F32),
            pltpu.VMEM((PLANE, 1, 3 * n_q * own), F32),
            pltpu.VMEM((1, 3 * n_q * own), F32),
            pltpu.VMEM((n_q, own, half), BF16),
            pltpu.VMEM((PLANE, CORES, own, half), BF16),
            pltpu.VMEM((n_p, own, half), BF16),
            pltpu.VMEM((Z, CORES, own, half), BF16),
            pltpu.VMEM((Z, 1, n_q * own), F32),
            pltpu.VMEM((1, n_q * own), F32),
            pltpu.SemaphoreType.DMA((9,)),
            pltpu.SemaphoreType.DMA((7,)),
            pltpu.SemaphoreType.DMA((7,)),
        ],
        compiler_params=pltpu.CompilerParams(
            collective_id=0, has_side_effects=True, vmem_limit_bytes=32 * 1024 * 1024),
    )(*(pltpu.with_memory_space_constraint(a, pltpu.HBM) for a in (queries, passages, positive)))
    return loss[0, 0], grads[0].astype(BF16), grads[1].astype(BF16)


def solution(mesh):
    placed = (P(("row", "col"), None), P(("row", "col"), None), P(("row", "col")))
    return jax.shard_map(
        per_device,
        mesh=mesh,
        in_specs=placed,
        out_specs=(P(), P(("row", "col"), None), P(("row", "col"), None)),
        check_vma=False,
    )
```

time: 40.5 us -> 34.3 us (0.85)
  Pallas kernels: 34.6 us -> 31.1 us
  local copies, waits for them, and re-layouts: 3.32 us -> 0.63 us
    pallas_call x1, Pallas kernels: 34.6 us -> 31.1 us  [per_device(): pl.pallas_call(functools.partial(kernel, n_q * own * Z), out_shape=(jax.S...]
    unnamed x8 -> x0, local copies, waits for them, and re-layouts: 3.32 us -> none
    squeeze x0 -> x1, local copies, waits for them, and re-layouts: none -> 0.63 us  [per_device(): return (loss[0, 0], grads[0].astype(BF16), grads[1].astype(BF16))]
where the time goes in v2:
time: 34.3 us; the launch traced here: 34.2 us
  Pallas kernels  31.1 us (91%)
  between operations  2.4 us (7%)
  local copies, waits for them, and re-layouts  0.63 us (2%)
    pallas_call x1, Pallas kernels, per_device(): pl.pallas_call(functools.partial(kernel, n_q * own * Z), out_shape=(jax.S...  31.1 us

profile of v2, /device:TPU:1, one launch (start us, length us, event | category | flops | bytes accessed | tf_op | source)
XLA Modules:
  0.0 34.2 jit_solution(16582416830545337613)
XLA Ops:
  0.6 31.1 %shard_map.58 = (f32[1,1]{1,0:T(1,128)}, bf16[2,4,2560]{2,1,0:T(4,128)(2,1)S(1)}) custom-call(bf16[4,2560]{1,0:T(4,128)(2,1)} %q_hbm.1, bf16[4,2560]{1,0:T(4,128)(2,1)} %p_hbm.1, s32[4]{0:T(128)} %pos_hbm.1), custom_call_target="tpu_custom_call" | custom-call | tf_op jit(solution)/shard_map/pallas_call | solution.py:212
  31.8 0.6 %slice_bitcast_fusion = (bf16[4,2560]{1,0:T(4,128)(2,1)}, bf16[4,2560]{1,0:T(4,128)(2,1)}) fusion(bf16[2,4,2560]{2,1,0:T(4,128)(2,1)S(1)} %get-tuple-element.6), kind=kLoop, calls=%fused_computation | loop fusion | bytes 81920 | tf_op jit(solution)/shard_map/squeeze | solution.py:245

commit v3 on v2

--- a/solution.py
+++ b/solution.py
@@ -24,38 +24,32 @@
 LINE_STEPS = sorted(range(1, Z), key=lambda s: -ring(s, Z))
 
 
-def device_of(x, y, z, core):
-    return (x * 2 + y % 2, z * 4 + (y // 2) * 2 + core)
-
-
-def kernel(total, q_hbm, p_hbm, pos_hbm, loss_ref, g_ref,
+def kernel(total, q_hbm, p_hbm, pos_hbm, g_ref,
            pos, stage, p_own, qbuf, pbuf, qwide, pwide, half_own, half_other, statbuf, stat_own,
            gq_send, gq_recv, gp_send, gp_recv, lossbuf, loss_own,
            local_sem, send_sem, recv_sem):
     row, col = lax.axis_index("row"), lax.axis_index("col")
-    x, z, core = row // 2, col // 4, col % 2
-    y = ((col // 2) % 2) * 2 + row % 2
+    x, z, core = row >> 1, col >> 2, col & 1
+    y = (col & 2) + (row & 1)
     chip = x * Y + y
     own = q_hbm.shape[0]
     half = q_hbm.shape[1] // CORES
     p_count, q_count = Z * CORES, PLANE * CORES
     q_slot, p_slot = chip * CORES + core, z * CORES + core
-    other = device_of(x, y, z, 1 - core)
-    plane = [((x + dx) % X, (y + dy) % Y) for dx, dy in PLANE_STEPS]
-    line = [(z + dz) % Z for dz in LINE_STEPS]
-
-    barrier = pltpu.get_barrier_semaphore()
-
-    def greet(device):
-        pl.semaphore_signal(barrier, inc=1, device_id=device, device_id_type=MESH)
-
-    for pz in line:
-        for c in range(CORES):
-            greet(device_of(x, y, pz, c))
-    for px, py in plane:
-        for c in range(CORES):
-            greet(device_of(px, py, z, c))
-    greet(other)
+    other = (row, col ^ 1)
+    xs, ys = [(x + d) & (X - 1) for d in range(X)], [(y + d) & (Y - 1) for d in range(Y)]
+    x_row, y_row = [px * 2 for px in xs], [py & 1 for py in ys]
+    y_col = [z * 4 + (py & 2) for py in ys]
+    x_slot, y_slot = [px * (Y * CORES) for px in xs], [py * CORES for py in ys]
+    zs = [(z + d) & (Z - 1) for d in range(Z)]
+    z_col, z_slot = [pz * 4 + (col & 2) for pz in zs], [pz * CORES for pz in zs]
+
+    def on_plane(step, c):
+        dx, dy = step
+        return (x_row[dx] + y_row[dy], y_col[dy] + c)
+
+    def on_line(step, c):
+        return (row, z_col[step] + c)
 
     loads = [pltpu.make_async_copy(pos_hbm, pos, local_sem.at[4])]
     for h in range(CORES):
@@ -64,6 +58,21 @@
         loads.append(pltpu.make_async_copy(q_hbm.at[:, part], stage.at[h, :, pl.ds(0, half)], local_sem.at[7 + h]))
     for load in loads:
         load.start()
+    barrier = pltpu.get_barrier_semaphore()
+
+    def greet(device):
+        pl.semaphore_signal(barrier, inc=1, device_id=device, device_id_type=MESH)
+
+    for far in range(X // 2 + Y // 2, 0, -1):
+        for c in range(CORES):
+            for step in LINE_STEPS:
+                if ring(step, Z) == far:
+                    greet(on_line(step, c))
+            for step in PLANE_STEPS:
+                if ring(step[0], X) + ring(step[1], Y) == far:
+                    greet(on_plane(step, c))
+    greet(other)
+
     loads[0].wait()
     lane = lax.broadcasted_iota(jnp.int32, (1, LANES), 1)
     codes = []
@@ -83,18 +92,12 @@
             src_ref=src, dst_ref=dst, send_sem=send_sem.at[kind], recv_sem=recv_sem.at[kind],
             device_id=to, device_id_type=MESH)
 
-    def gather_plane(px, py):
-        for c in range(CORES):
-            send(stage.at[c], qbuf.at[q_slot], device_of(px, py, z, c), 0).start()
-
-    def gather_line(pz):
-        for c in range(CORES):
-            send(p_own.at[c], pbuf.at[p_slot], device_of(x, y, pz, c), 1).start()
-
     for k in range(PLANE - 1):
-        gather_plane(*plane[k])
+        for c in range(CORES):
+            send(stage.at[c], qbuf.at[q_slot], on_plane(PLANE_STEPS[k], c), 0).start()
         if k % 2 == 0 and k // 2 < Z - 1:
-            gather_line(line[k // 2])
+            for c in range(CORES):
+                send(p_own.at[c], pbuf.at[p_slot], on_line(LINE_STEPS[k // 2], c), 1).start()
     send(stage.at[1 - core], qbuf.at[q_slot], other, 0).start()
     send(p_own.at[1 - core], pbuf.at[p_slot], other, 1).start()
     own_q = pltpu.make_async_copy(stage.at[core], qbuf.at[q_slot], local_sem.at[0])
@@ -110,8 +113,8 @@
 
     n_p = p_count * own
     slot = lax.broadcasted_iota(jnp.int32, (n_p, LANES), 0)
-    p_row, p_col = device_of(x, y, slot // (CORES * own), (slot // own) % CORES)
-    p_id = (p_row * 32 + p_col) * own + slot % own
+    p_col = slot // (CORES * own) * 4 + (col & 2) + (slot // own) % CORES
+    p_id = (row * 32 + p_col) * own + slot % own
     p_lane = lax.broadcasted_iota(jnp.int32, (n_p, LANES), 1)
     p_code = ((p_lane == p_id // 32) | (p_lane == 32 + p_id % 32)).astype(F32).astype(BF16)
 
@@ -141,8 +144,8 @@
     stat_own[:, n_q:2 * n_q] = jnp.sum(jnp.exp(scores - peak), axis=0, keepdims=True)
     stat_own[:, 2 * n_q:] = jnp.sum(jnp.where(matched, scores, 0.0), axis=0, keepdims=True)
     statbuf[pl.ds(chip, 1)] = stat_own[...][None]
-    for px, py in plane:
-        send(stat_own, statbuf.at[chip], device_of(px, py, z, core), 3).start()
+    for step in PLANE_STEPS:
+        send(stat_own, statbuf.at[chip], on_plane(step, core), 3).start()
     wait_recv(statbuf.at[pl.ds(0, PLANE - 1)], 3)
     stats = statbuf[...]
     peaks, sums, picks = stats[:, :, :n_q], stats[:, :, n_q:2 * n_q], stats[:, :, 2 * n_q:]
@@ -153,33 +156,36 @@
 
     loss_own[...] = row_peak + jnp.log(totals) - positive_score
     lossbuf[pl.ds(z, 1)] = loss_own[...][None]
-    for pz in line:
-        send(loss_own, lossbuf.at[z], device_of(x, y, pz, core), 6).start()
+    for step in LINE_STEPS:
+        send(loss_own, lossbuf.at[z], on_line(step, core), 6).start()
+
+    for at in range(0, half, 256):
+        part = jnp.dot(weights, queries[:, at:at + 256], preferred_element_type=F32).astype(BF16)
+        for s in range(p_count):
+            gp_send[s, :, at:at + 256] = part[s * own:(s + 1) * own]
+    for step in LINE_STEPS:
+        for c in range(CORES):
+            send(gp_send.at[z_slot[step] + c], gp_recv.at[z, core], on_line(step, c), 5).start()
+    send(gp_send.at[z * CORES + 1 - core], gp_recv.at[z, core], other, 5).start()
+    own_gp = pltpu.make_async_copy(gp_send.at[p_slot], gp_recv.at[z, core], local_sem.at[3])
+    own_gp.start()
 
     for at in range(0, half, 256):
         part = lax.dot_general(weights, passages[:, at:at + 256], (((0,), (0,)), ((), ())),
                                preferred_element_type=F32).astype(BF16)
         for s in range(q_count):
             gq_send[s, :, at:at + 256] = part[s * own:(s + 1) * own]
-    for px, py in plane:
-        for c in range(CORES):
-            send(gq_send.at[(px * Y + py) * CORES + c], gq_recv.at[chip, core], device_of(px, py, z, c), 4).start()
+    for step in PLANE_STEPS:
+        for c in range(CORES):
+            send(gq_send.at[x_slot[step[0]] + y_slot[step[1]] + c], gq_recv.at[chip, core], on_plane(step, c), 4).start()
     send(gq_send.at[chip * CORES + 1 - core], gq_recv.at[chip, core], other, 4).start()
     own_gq = pltpu.make_async_copy(gq_send.at[q_slot], gq_recv.at[chip, core], local_sem.at[2])
     own_gq.start()
-    for at in range(0, half, 256):
-        part = jnp.dot(weights, queries[:, at:at + 256], preferred_element_type=F32).astype(BF16)
-        for s in range(p_count):
-            gp_send[s, :, at:at + 256] = part[s * own:(s + 1) * own]
-    for pz in line:
-        for c in range(CORES):
-            send(gp_send.at[pz * CORES + c], gp_recv.at[z, core], device_of(x, y, pz, c), 5).start()
-    send(gp_send.at[z * CORES + 1 - core], gp_recv.at[z, core], other, 5).start()
-    own_gp = pltpu.make_async_copy(gp_send.at[p_slot], gp_recv.at[z, core], local_sem.at[3])
-    own_gp.start()
-
     wait_recv(lossbuf.at[pl.ds(0, Z - 1)], 6)
-    loss_ref[0, 0] = jnp.sum(jnp.sum(lossbuf[...], axis=0)) / total
+    loss = jnp.sum(jnp.sum(lossbuf[...], axis=0)) / total
+    at_first = (lax.broadcasted_iota(jnp.int32, (own, LANES), 0) == 0) & (lax.broadcasted_iota(jnp.int32, (own, LANES), 1) == 0)
+    g_ref[2] = jnp.zeros(g_ref.shape[1:], F32)
+    g_ref[2, :, :LANES] = jnp.where(at_first, loss, 0.0)
 
     own_gq.wait()
     wait_recv(gq_send.at[pl.ds(0, q_count - 1)], 4)
@@ -187,14 +193,14 @@
         acc = gq_recv[0, h].astype(F32)
         for k in range(1, PLANE):
             acc += gq_recv[k, h].astype(F32)
-        g_ref[0, :, h * half:(h + 1) * half] = acc.astype(BF16)
+        g_ref[0, :, h * half:(h + 1) * half] = acc
     own_gp.wait()
     wait_recv(gp_send.at[pl.ds(0, p_count - 1)], 5)
     for h in range(CORES):
         acc = gp_recv[0, h].astype(F32)
         for k in range(1, Z):
             acc += gp_recv[k, h].astype(F32)
-        g_ref[1, :, h * half:(h + 1) * half] = acc.astype(BF16)
+        g_ref[1, :, h * half:(h + 1) * half] = acc
 
     wait_send(qbuf.at[pl.ds(0, q_count - 1)], 0)
     wait_send(pbuf.at[pl.ds(0, p_count - 1)], 1)
@@ -204,19 +210,26 @@
     wait_send(lossbuf.at[pl.ds(0, Z - 1)], 6)
 
 
+def hand_out(all_ref, loss_out, gq_out, gp_out, narrow, sem):
+    narrow[...] = all_ref[:2].astype(BF16)
+    copies = (pltpu.make_async_copy(all_ref.at[2, pl.ds(0, 1), pl.ds(0, LANES)], loss_out, sem.at[2]),
+              pltpu.make_async_copy(narrow.at[0], gq_out, sem.at[0]), pltpu.make_async_copy(narrow.at[1], gp_out, sem.at[1]))
+    for copy in copies:
+        copy.start()
+    for copy in copies:
+        copy.wait()
+
+
 def per_device(queries, passages, positive):
     own, width = queries.shape
     half = width // CORES
     n_q, n_p = PLANE * CORES, Z * CORES
     vmem, hbm = pl.BlockSpec(memory_space=pltpu.VMEM), pl.BlockSpec(memory_space=pltpu.HBM)
-    loss, grads = pl.pallas_call(
+    out = pl.pallas_call(
         functools.partial(kernel, n_q * own * Z),
-        out_shape=(
-            jax.ShapeDtypeStruct((1, 1), F32),
-            jax.ShapeDtypeStruct((2, own, width), BF16),
-        ),
+        out_shape=jax.ShapeDtypeStruct((3, own, width), F32),
         in_specs=[hbm, hbm, hbm],
-        out_specs=(pl.BlockSpec(memory_space=pltpu.SMEM), vmem),
+        out_specs=vmem,
         scratch_shapes=[
             pltpu.SMEM((own,), jnp.int32),
             pltpu.VMEM((CORES, own, half + LANES), BF16),
@@ -242,7 +255,18 @@
         compiler_params=pltpu.CompilerParams(
             collective_id=0, has_side_effects=True, vmem_limit_bytes=32 * 1024 * 1024),
     )(*(pltpu.with_memory_space_constraint(a, pltpu.HBM) for a in (queries, passages, positive)))
-    return loss[0, 0], grads[0].astype(BF16), grads[1].astype(BF16)
+    loss, gq, gp = pl.pallas_call(
+        hand_out,
+        out_shape=(
+            jax.ShapeDtypeStruct((1, LANES), F32),
+            jax.ShapeDtypeStruct((own, width), BF16),
+            jax.ShapeDtypeStruct((own, width), BF16),
+        ),
+        in_specs=[vmem],
+        out_specs=(hbm, hbm, hbm),
+        scratch_shapes=[pltpu.VMEM((2, own, width), BF16), pltpu.SemaphoreType.DMA((3,))],
+    )(pltpu.with_memory_space_constraint(out, pltpu.VMEM))
+    return loss[0, 0], gq, gp
 
 
 def solution(mesh):

time: 34.3 us -> 31.6 us (0.921)
  between operations: 2.4 us -> 0.64 us
  local copies, waits for them, and re-layouts: 0.63 us -> 0 us
    squeeze x1 -> x0, local copies, waits for them, and re-layouts: 0.63 us -> none  [per_device(): return (loss[0, 0], grads[0].astype(BF16), grads[1].astype(BF16))]
    pallas_call x1 -> x2, Pallas kernels: 31.1 us -> 30.9 us  [the longest x1 30.2 us: per_device(): pl.pallas_call(functools.partial(kernel, n_q * own * Z), out_shape=jax.Sh...]
where the time goes in v3:
time: 31.6 us; the launch traced here: 31.5 us
  Pallas kernels  30.9 us (98%)
  between operations  0.64 us (2%)
    pallas_call x1, Pallas kernels, per_device(): pl.pallas_call(functools.partial(kernel, n_q * own * Z), out_shape=jax.Sh...  30.2 us
    pallas_call x1, Pallas kernels, per_device(): pl.pallas_call(hand_out, out_shape=(jax.ShapeDtypeStruct((1, LANES), F32)...  0.65 us

profile of v3, /device:TPU:1, one launch (start us, length us, event | category | flops | bytes accessed | tf_op | source)
XLA Modules:
  0.0 31.5 jit_solution(17745407725753256701)
XLA Ops:
  0.6 30.2 %shard_map.58.all_ref = f32[3,4,2560]{2,1,0:T(4,128)S(1)} custom-call(bf16[4,2560]{1,0:T(4,128)(2,1)} %q_hbm.1, bf16[4,2560]{1,0:T(4,128)(2,1)} %p_hbm.1, s32[4]{0:T(128)} %pos_hbm.1), custom_call_target="tpu_custom_call" | custom-call | tf_op jit(solution)/shard_map/pallas_call | solution.py:228
  30.9 0.7 %shard_map.59 = (f32[1,128]{1,0:T(1,128)}, bf16[4,2560]{1,0:T(4,128)(2,1)}, bf16[4,2560]{1,0:T(4,128)(2,1)}) custom-call(f32[3,4,2560]{2,1,0:T(4,128)S(1)} %shard_map.58.all_ref), custom_call_target="tpu_custom_call" | custom-call | tf_op jit(solution)/shard_map/pallas_call | solution.py:258

commit v4 on v3

--- a/solution.py
+++ b/solution.py
@@ -34,8 +34,8 @@
     chip = x * Y + y
     own = q_hbm.shape[0]
     half = q_hbm.shape[1] // CORES
-    p_count, q_count = Z * CORES, PLANE * CORES
-    q_slot, p_slot = chip * CORES + core, z * CORES + core
+    q_count, p_count = Z * CORES, PLANE * CORES
+    p_slot, q_slot = chip * CORES + core, z * CORES + core
     other = (row, col ^ 1)
     xs, ys = [(x + d) & (X - 1) for d in range(X)], [(y + d) & (Y - 1) for d in range(Y)]
     x_row, y_row = [px * 2 for px in xs], [py & 1 for py in ys]
@@ -94,10 +94,10 @@
 
     for k in range(PLANE - 1):
         for c in range(CORES):
-            send(stage.at[c], qbuf.at[q_slot], on_plane(PLANE_STEPS[k], c), 0).start()
+            send(p_own.at[c], pbuf.at[p_slot], on_plane(PLANE_STEPS[k], c), 1).start()
         if k % 2 == 0 and k // 2 < Z - 1:
             for c in range(CORES):
-                send(p_own.at[c], pbuf.at[p_slot], on_line(LINE_STEPS[k // 2], c), 1).start()
+                send(stage.at[c], qbuf.at[q_slot], on_line(LINE_STEPS[k // 2], c), 0).start()
     send(stage.at[1 - core], qbuf.at[q_slot], other, 0).start()
     send(p_own.at[1 - core], pbuf.at[p_slot], other, 1).start()
     own_q = pltpu.make_async_copy(stage.at[core], qbuf.at[q_slot], local_sem.at[0])
@@ -113,8 +113,10 @@
 
     n_p = p_count * own
     slot = lax.broadcasted_iota(jnp.int32, (n_p, LANES), 0)
-    p_col = slot // (CORES * own) * 4 + (col & 2) + (slot // own) % CORES
-    p_id = (row * 32 + p_col) * own + slot % own
+    p_chip = slot // (CORES * own)
+    p_row = p_chip // Y * 2 + p_chip % 2
+    p_col = z * 4 + p_chip % Y // 2 * 2 + slot // own % CORES
+    p_id = (p_row * 32 + p_col) * own + slot % own
     p_lane = lax.broadcasted_iota(jnp.int32, (n_p, LANES), 1)
     p_code = ((p_lane == p_id // 32) | (p_lane == 32 + p_id % 32)).astype(F32).astype(BF16)
 
@@ -141,47 +143,48 @@
     n_q = q_count * own
     peak = jnp.max(scores, axis=0, keepdims=True)
     stat_own[:, :n_q] = peak
-    stat_own[:, n_q:2 * n_q] = jnp.sum(jnp.exp(scores - peak), axis=0, keepdims=True)
-    stat_own[:, 2 * n_q:] = jnp.sum(jnp.where(matched, scores, 0.0), axis=0, keepdims=True)
-    statbuf[pl.ds(chip, 1)] = stat_own[...][None]
-    for step in PLANE_STEPS:
-        send(stat_own, statbuf.at[chip], on_plane(step, core), 3).start()
-    wait_recv(statbuf.at[pl.ds(0, PLANE - 1)], 3)
+    stat_own[:, LANES:LANES + n_q] = jnp.sum(jnp.exp(scores - peak), axis=0, keepdims=True)
+    stat_own[:, 2 * LANES:2 * LANES + n_q] = jnp.sum(jnp.where(matched, scores, 0.0), axis=0, keepdims=True)
+    statbuf[pl.ds(z, 1)] = stat_own[...][None]
+    for step in LINE_STEPS:
+        send(stat_own, statbuf.at[z], on_line(step, core), 3).start()
+    wait_recv(statbuf.at[pl.ds(0, Z - 1)], 3)
     stats = statbuf[...]
-    peaks, sums, picks = stats[:, :, :n_q], stats[:, :, n_q:2 * n_q], stats[:, :, 2 * n_q:]
+    peaks, sums, picks = stats[:, :, :n_q], stats[:, :, LANES:LANES + n_q], stats[:, :, 2 * LANES:2 * LANES + n_q]
     row_peak = jnp.max(peaks, axis=0)
     totals = jnp.sum(sums * jnp.exp(peaks - row_peak[None]), axis=0)
     positive_score = jnp.sum(picks, axis=0)
     weights = (jnp.exp(scores - row_peak) / totals - matched.astype(F32)).astype(BF16)
 
-    loss_own[...] = row_peak + jnp.log(totals) - positive_score
-    lossbuf[pl.ds(z, 1)] = loss_own[...][None]
-    for step in LINE_STEPS:
-        send(loss_own, lossbuf.at[z], on_line(step, core), 6).start()
+    loss_own[...] = jnp.zeros_like(loss_own)
+    loss_own[:, :n_q] = row_peak + jnp.log(totals) - positive_score
+    lossbuf[pl.ds(chip, 1)] = loss_own[...][None]
+    for step in PLANE_STEPS:
+        send(loss_own, lossbuf.at[chip], on_plane(step, core), 6).start()
 
     for at in range(0, half, 256):
         part = jnp.dot(weights, queries[:, at:at + 256], preferred_element_type=F32).astype(BF16)
         for s in range(p_count):
             gp_send[s, :, at:at + 256] = part[s * own:(s + 1) * own]
-    for step in LINE_STEPS:
-        for c in range(CORES):
-            send(gp_send.at[z_slot[step] + c], gp_recv.at[z, core], on_line(step, c), 5).start()
-    send(gp_send.at[z * CORES + 1 - core], gp_recv.at[z, core], other, 5).start()
-    own_gp = pltpu.make_async_copy(gp_send.at[p_slot], gp_recv.at[z, core], local_sem.at[3])
+    for step in PLANE_STEPS:
+        for c in range(CORES):
+            send(gp_send.at[x_slot[step[0]] + y_slot[step[1]] + c], gp_recv.at[chip, core], on_plane(step, c), 5).start()
+    send(gp_send.at[chip * CORES + 1 - core], gp_recv.at[chip, core], other, 5).start()
+    own_gp = pltpu.make_async_copy(gp_send.at[p_slot], gp_recv.at[chip, core], local_sem.at[3])
     own_gp.start()
-
     for at in range(0, half, 256):
         part = lax.dot_general(weights, passages[:, at:at + 256], (((0,), (0,)), ((), ())),
                                preferred_element_type=F32).astype(BF16)
         for s in range(q_count):
             gq_send[s, :, at:at + 256] = part[s * own:(s + 1) * own]
-    for step in PLANE_STEPS:
-        for c in range(CORES):
-            send(gq_send.at[x_slot[step[0]] + y_slot[step[1]] + c], gq_recv.at[chip, core], on_plane(step, c), 4).start()
-    send(gq_send.at[chip * CORES + 1 - core], gq_recv.at[chip, core], other, 4).start()
-    own_gq = pltpu.make_async_copy(gq_send.at[q_slot], gq_recv.at[chip, core], local_sem.at[2])
+    for step in LINE_STEPS:
+        for c in range(CORES):
+            send(gq_send.at[z_slot[step] + c], gq_recv.at[z, core], on_line(step, c), 4).start()
+    send(gq_send.at[z * CORES + 1 - core], gq_recv.at[z, core], other, 4).start()
+    own_gq = pltpu.make_async_copy(gq_send.at[q_slot], gq_recv.at[z, core], local_sem.at[2])
     own_gq.start()
-    wait_recv(lossbuf.at[pl.ds(0, Z - 1)], 6)
+
+    wait_recv(lossbuf.at[pl.ds(0, PLANE - 1)], 6)
     loss = jnp.sum(jnp.sum(lossbuf[...], axis=0)) / total
     at_first = (lax.broadcasted_iota(jnp.int32, (own, LANES), 0) == 0) & (lax.broadcasted_iota(jnp.int32, (own, LANES), 1) == 0)
     g_ref[2] = jnp.zeros(g_ref.shape[1:], F32)
@@ -191,23 +194,23 @@
     wait_recv(gq_send.at[pl.ds(0, q_count - 1)], 4)
     for h in range(CORES):
         acc = gq_recv[0, h].astype(F32)
-        for k in range(1, PLANE):
+        for k in range(1, Z):
             acc += gq_recv[k, h].astype(F32)
         g_ref[0, :, h * half:(h + 1) * half] = acc
     own_gp.wait()
     wait_recv(gp_send.at[pl.ds(0, p_count - 1)], 5)
     for h in range(CORES):
         acc = gp_recv[0, h].astype(F32)
-        for k in range(1, Z):
+        for k in range(1, PLANE):
             acc += gp_recv[k, h].astype(F32)
         g_ref[1, :, h * half:(h + 1) * half] = acc
 
     wait_send(qbuf.at[pl.ds(0, q_count - 1)], 0)
     wait_send(pbuf.at[pl.ds(0, p_count - 1)], 1)
-    wait_send(statbuf.at[pl.ds(0, PLANE - 1)], 3)
+    wait_send(statbuf.at[pl.ds(0, Z - 1)], 3)
     wait_send(gq_send.at[pl.ds(0, q_count - 1)], 4)
     wait_send(gp_send.at[pl.ds(0, p_count - 1)], 5)
-    wait_send(lossbuf.at[pl.ds(0, Z - 1)], 6)
+    wait_send(lossbuf.at[pl.ds(0, PLANE - 1)], 6)
 
 
 def hand_out(all_ref, loss_out, gq_out, gp_out, narrow, sem):
@@ -223,10 +226,10 @@
 def per_device(queries, passages, positive):
     own, width = queries.shape
     half = width // CORES
-    n_q, n_p = PLANE * CORES, Z * CORES
+    n_q, n_p = Z * CORES, PLANE * CORES
     vmem, hbm = pl.BlockSpec(memory_space=pltpu.VMEM), pl.BlockSpec(memory_space=pltpu.HBM)
     out = pl.pallas_call(
-        functools.partial(kernel, n_q * own * Z),
+        functools.partial(kernel, n_q * own * PLANE),
         out_shape=jax.ShapeDtypeStruct((3, own, width), F32),
         in_specs=[hbm, hbm, hbm],
         out_specs=vmem,
@@ -240,14 +243,14 @@
             pltpu.VMEM((n_p * own, half), F32),
             pltpu.VMEM((n_p * own, n_q * own), F32),
             pltpu.VMEM((n_p * own, n_q * own), F32),
-            pltpu.VMEM((PLANE, 1, 3 * n_q * own), F32),
-            pltpu.VMEM((1, 3 * n_q * own), F32),
+            pltpu.VMEM((Z, 1, 3 * LANES), F32),
+            pltpu.VMEM((1, 3 * LANES), F32),
             pltpu.VMEM((n_q, own, half), BF16),
+            pltpu.VMEM((Z, CORES, own, half), BF16),
+            pltpu.VMEM((n_p, own, half), BF16),
             pltpu.VMEM((PLANE, CORES, own, half), BF16),
-            pltpu.VMEM((n_p, own, half), BF16),
-            pltpu.VMEM((Z, CORES, own, half), BF16),
-            pltpu.VMEM((Z, 1, n_q * own), F32),
-            pltpu.VMEM((1, n_q * own), F32),
+            pltpu.VMEM((PLANE, 1, LANES), F32),
+            pltpu.VMEM((1, LANES), F32),
             pltpu.SemaphoreType.DMA((9,)),
             pltpu.SemaphoreType.DMA((7,)),
             pltpu.SemaphoreType.DMA((7,)),

time: 31.6 us -> 31.4 us (level)
  no operation moved by 1% of the time
where the time goes in v4:
time: 31.4 us; the launch traced here: 31.3 us
  Pallas kernels  30.6 us (97%)
  between operations  0.64 us (2%)
    pallas_call x1, Pallas kernels, per_device(): pl.pallas_call(functools.partial(kernel, n_q * own * PLANE), out_shape=ja...  30 us
    pallas_call x1, Pallas kernels, per_device(): pl.pallas_call(hand_out, out_shape=(jax.ShapeDtypeStruct((1, LANES), F32)...  0.65 us

profile of v4, /device:TPU:1, one launch (start us, length us, event | category | flops | bytes accessed | tf_op | source)
XLA Modules:
  0.0 31.3 jit_solution(16008135930253755634)
XLA Ops:
  0.6 30.0 %shard_map.58.all_ref = f32[3,4,2560]{2,1,0:T(4,128)S(1)} custom-call(bf16[4,2560]{1,0:T(4,128)(2,1)} %q_hbm.1, bf16[4,2560]{1,0:T(4,128)(2,1)} %p_hbm.1, s32[4]{0:T(128)} %pos_hbm.1), custom_call_target="tpu_custom_call" | custom-call | tf_op jit(solution)/shard_map/pallas_call | solution.py:231
  30.6 0.7 %shard_map.59 = (f32[1,128]{1,0:T(1,128)}, bf16[4,2560]{1,0:T(4,128)(2,1)}, bf16[4,2560]{1,0:T(4,128)(2,1)}) custom-call(f32[3,4,2560]{2,1,0:T(4,128)S(1)} %shard_map.58.all_ref), custom_call_target="tpu_custom_call" | custom-call | tf_op jit(solution)/shard_map/pallas_call | solution.py:261

commit v5 on v4

v5 whole, which is shorter than its diff:
```python
import functools

import jax
import jax.numpy as jnp
from jax import lax
from jax.experimental import pallas as pl
from jax.experimental.pallas import tpu as pltpu
from jax.sharding import PartitionSpec as P

MESH = pl.DeviceIdType.MESH
X, Y, Z, CORES = 4, 4, 8, 2
PLANE = X * Y
LANES = 128
F32, BF16 = jnp.float32, jnp.bfloat16


def ring(step, n):
    return min(step, n - step)


PLANE_STEPS = sorted(
    ((dx, dy) for dx in range(X) for dy in range(Y) if dx or dy),
    key=lambda s: -(ring(s[0], X) + ring(s[1], Y)))
LINE_STEPS = sorted(range(1, Z), key=lambda s: -ring(s, Z))


def kernel(total, q_hbm, p_hbm, pos_hbm, g_ref,
           pos, stage, p_own, qbuf, pbuf, qwide, pwide, statbuf, stat_own,
           gp_send, gp_recv, p_other, score_own, score_other, gq_send, gq_recv, lossbuf, loss_own,
           local_sem, send_sem, recv_sem, land_sem):
    row, col = lax.axis_index("row"), lax.axis_index("col")
    x, z, core = row >> 1, col >> 2, col & 1
    y = (col & 2) + (row & 1)
    chip = x * Y + y
    own, width = q_hbm.shape
    half = width // 2
    q_slot = core * Z + z
    other = (row, col ^ 1)
    xs, ys = [(x + d) & (X - 1) for d in range(X)], [(y + d) & (Y - 1) for d in range(Y)]
    x_row, y_row = [px * 2 for px in xs], [py & 1 for py in ys]
    y_col = [z * 4 + (py & 2) for py in ys]
    x_slot = [px * Y for px in xs]
    zs = [(z + d) & (Z - 1) for d in range(Z)]
    z_col = [pz * 4 + (col & 2) for pz in zs]

    def on_plane(step):
        dx, dy = step
        return (x_row[dx] + y_row[dy], y_col[dy] + core)

    def on_line(step, c):
        return (row, z_col[step] + c)

    loads = [
        pltpu.make_async_copy(pos_hbm, pos, local_sem.at[0]),
        pltpu.make_async_copy(p_hbm, p_own, local_sem.at[1]),
        pltpu.make_async_copy(q_hbm, stage.at[:, pl.ds(0, width)], local_sem.at[2]),
    ]
    for load in loads:
        load.start()
    barrier = pltpu.get_barrier_semaphore()

    def greet(device):
        pl.semaphore_signal(barrier, inc=1, device_id=device, device_id_type=MESH)

    for far in range(X // 2 + Y // 2, 0, -1):
        for step in PLANE_STEPS:
            if ring(step[0], X) + ring(step[1], Y) == far:
                greet(on_plane(step))
        for step in LINE_STEPS:
            if ring(step, Z) == far:
                for c in range(CORES):
                    greet(on_line(step, c))
    greet(other)

    loads[0].wait()
    lane = lax.broadcasted_iota(jnp.int32, (1, LANES), 1)
    codes = []
    for k in range(own):
        index = pos[k]
        codes.append(((lane == index // 32) | (lane == 32 + index % 32)).astype(F32))
    code = jnp.concatenate(codes, axis=0).astype(BF16)
    for load in loads[1:]:
        load.wait()
    stage[:, width:] = code

    pl.semaphore_wait(barrier, PLANE - 1 + (Z - 1) * CORES + 1)

    def send(src, dst, to, kind, landed=None):
        return pltpu.make_async_remote_copy(
            src_ref=src, dst_ref=dst, send_sem=send_sem.at[kind],
            recv_sem=recv_sem.at[kind] if landed is None else landed,
            device_id=to, device_id_type=MESH)

    for step in LINE_STEPS:
        send(stage, qbuf.at[q_slot], on_line(step, core), 0, land_sem.at[step]).start()
    for step in PLANE_STEPS:
        send(p_own, pbuf.at[chip], on_plane(step), 1).start()
    send(stage, qbuf.at[q_slot], other, 2).start()
    own_q = pltpu.make_async_copy(stage, qbuf.at[q_slot], local_sem.at[3])
    own_p = pltpu.make_async_copy(p_own, pbuf.at[chip], local_sem.at[4])
    own_q.start()
    own_p.start()

    def wait_recv(ref, kind):
        pltpu.make_async_copy(ref, ref, recv_sem.at[kind]).wait()

    def wait_send(ref, kind):
        pltpu.make_async_copy(ref, ref, send_sem.at[kind]).wait()

    p_count, q_count = PLANE, Z * CORES
    n_p, n_q = p_count * own, q_count * own
    slot = lax.broadcasted_iota(jnp.int32, (n_p, LANES), 0)
    p_chip = slot // own
    p_row = p_chip // Y * 2 + p_chip % 2
    p_lane = lax.broadcasted_iota(jnp.int32, (n_p, LANES), 1)

    def passage_code(c):
        p_id = (p_row * 32 + z * 4 + p_chip % Y // 2 * 2 + c) * own + slot % own
        return ((p_lane == p_id // 32) | (p_lane == 32 + p_id % 32)).astype(F32).astype(BF16)

    for step in LINE_STEPS[::-1]:
        landed = qbuf.at[core * Z + zs[Z - step]]
        pltpu.make_async_copy(landed, landed, land_sem.at[step]).wait()
        send(landed, landed, other, 2).start()
    own_p.wait()
    own_q.wait()
    wait_recv(pbuf.at[pl.ds(0, p_count - 1)], 1)
    give_passages = send(pbuf, p_other, other, 7)
    give_passages.start()
    for s in range(p_count):
        pwide[s * own:(s + 1) * own, :] = pbuf[s].astype(F32)
    passages = pwide[...].astype(BF16)
    wait_recv(qbuf.at[pl.ds(0, Z)], 2)
    for s in range(q_count):
        qwide[s * own:(s + 1) * own, :] = qbuf[s].astype(F32)
    queries = qwide[:, :width].astype(BF16)
    q_code = qwide[:, width:].astype(BF16)

    contract_last = (((1,), (1,)), ((), ()))
    scores = lax.dot_general(passages, queries, contract_last, preferred_element_type=F32)

    def match(c):
        return lax.dot_general(passage_code(c), q_code, contract_last, preferred_element_type=F32) > 1.5

    matched = match(core)

    peak = jnp.max(scores, axis=0, keepdims=True)
    stat_own[:, :n_q] = peak
    stat_own[:, LANES:LANES + n_q] = jnp.sum(jnp.exp(scores - peak), axis=0, keepdims=True)
    stat_own[:, 2 * LANES:2 * LANES + n_q] = jnp.sum(jnp.where(matched, scores, 0.0), axis=0, keepdims=True)
    statbuf[pl.ds(q_slot, 1)] = stat_own[...][None]
    for step in LINE_STEPS:
        for c in range(CORES):
            send(stat_own, statbuf.at[q_slot], on_line(step, c), 3).start()
    send(stat_own, statbuf.at[q_slot], other, 3).start()
    score_own[...] = scores
    give_scores = send(score_own, score_other, other, 8)
    give_scores.start()
    matched_other = match(1 - core)
    give_passages.wait()
    for s in range(p_count):
        pwide[s * own:(s + 1) * own, :] = p_other[s].astype(F32)
    passages_other = pwide[...].astype(BF16)
    give_scores.wait()
    wait_recv(statbuf.at[pl.ds(0, q_count - 1)], 3)
    stats = statbuf[...]
    peaks, sums, picks = stats[:, :, :n_q], stats[:, :, LANES:LANES + n_q], stats[:, :, 2 * LANES:2 * LANES + n_q]
    row_peak = jnp.max(peaks, axis=0)
    totals = jnp.sum(sums * jnp.exp(peaks - row_peak[None]), axis=0)
    positive_score = jnp.sum(picks, axis=0)

    def weigh(block, match):
        return jnp.exp(block - row_peak) / totals - match.astype(F32)

    wide = weigh(scores, matched)
    weights = wide.astype(BF16)

    loss_own[...] = jnp.zeros_like(loss_own)
    loss_own[:, :n_q] = row_peak + jnp.log(totals) - positive_score
    lossbuf[pl.ds(chip, 1)] = loss_own[...][None]
    for step in PLANE_STEPS:
        send(loss_own, lossbuf.at[chip], on_plane(step), 6).start()
    for at in range(0, width, 256):
        part = jnp.dot(weights, queries[:, at:at + 256], preferred_element_type=F32).astype(BF16)
        for s in range(p_count):
            gp_send[s, :, at:at + 256] = part[s * own:(s + 1) * own]
    for step in PLANE_STEPS:
        send(gp_send.at[x_slot[step[0]] + ys[step[1]]], gp_recv.at[chip], on_plane(step), 4).start()
    own_gp = pltpu.make_async_copy(gp_send.at[chip], gp_recv.at[chip], local_sem.at[5])
    own_gp.start()

    def of_mine(w):
        return jnp.where(core == 0, w[:, :n_q // 2], w[:, n_q // 2:]).astype(BF16)

    w_own, w_other = of_mine(wide), of_mine(weigh(score_other[...], matched_other))

    def share(w, block):
        return lax.dot_general(w, block, (((0,), (0,)), ((), ())), preferred_element_type=F32)

    for at in range(0, width, 256):
        part = (share(w_own, passages[:, at:at + 256]) + share(w_other, passages_other[:, at:at + 256])).astype(BF16)
        for s in range(Z):
            gq_send[s, :, at:at + 256] = part[s * own:(s + 1) * own]
    for step in LINE_STEPS:
        send(gq_send.at[zs[step]], gq_recv.at[z], on_line(step, core), 5).start()
    own_gq = pltpu.make_async_copy(gq_send.at[z], gq_recv.at[z], local_sem.at[6])
    own_gq.start()

    wait_recv(lossbuf.at[pl.ds(0, PLANE - 1)], 6)
    loss = jnp.sum(jnp.sum(lossbuf[...], axis=0)) / total
    at_first = (lax.broadcasted_iota(jnp.int32, (own, LANES), 0) == 0) & (lax.broadcasted_iota(jnp.int32, (own, LANES), 1) == 0)
    g_ref[2] = jnp.zeros(g_ref.shape[1:], F32)
    g_ref[2, :, :LANES] = jnp.where(at_first, loss, 0.0)

    own_gp.wait()
    wait_recv(gp_send.at[pl.ds(0, p_count - 1)], 4)
    for h in range(2):
        part = slice(h * half, (h + 1) * half)
        acc = gp_recv[0, :, part].astype(F32)
        for k in range(1, PLANE):
            acc += gp_recv[k, :, part].astype(F32)
        g_ref[1, :, part] = acc
    own_gq.wait()
    wait_recv(gq_send.at[pl.ds(0, Z - 1)], 5)
    for h in range(2):
        part = slice(h * half, (h + 1) * half)
        acc = gq_recv[0, :, part].astype(F32)
        for k in range(1, Z):
            acc += gq_recv[k, :, part].astype(F32)
        g_ref[0, :, part] = acc

    wait_send(qbuf.at[pl.ds(0, Z - 1)], 0)
    wait_send(pbuf.at[pl.ds(0, p_count - 1)], 1)
    wait_send(qbuf.at[pl.ds(0, Z)], 2)
    wait_send(statbuf.at[pl.ds(0, q_count - 1)], 3)
    wait_send(gp_send.at[pl.ds(0, p_count - 1)], 4)
    wait_send(gq_send.at[pl.ds(0, Z - 1)], 5)
    wait_send(lossbuf.at[pl.ds(0, PLANE - 1)], 6)


def hand_out(all_ref, loss_out, gq_out, gp_out, narrow, sem):
    narrow[...] = all_ref[:2].astype(BF16)
    copies = (pltpu.make_async_copy(all_ref.at[2, pl.ds(0, 1), pl.ds(0, LANES)], loss_out, sem.at[2]),
              pltpu.make_async_copy(narrow.at[0], gq_out, sem.at[0]), pltpu.make_async_copy(narrow.at[1], gp_out, sem.at[1]))
    for copy in copies:
        copy.start()
    for copy in copies:
        copy.wait()


def per_device(queries, passages, positive):
    own, width = queries.shape
    n_q, n_p = Z * CORES, PLANE
    vmem, hbm = pl.BlockSpec(memory_space=pltpu.VMEM), pl.BlockSpec(memory_space=pltpu.HBM)
    out = pl.pallas_call(
        functools.partial(kernel, n_q * own * PLANE),
        out_shape=jax.ShapeDtypeStruct((3, own, width), F32),
        in_specs=[hbm, hbm, hbm],
        out_specs=vmem,
        scratch_shapes=[
            pltpu.SMEM((own,), jnp.int32),
            pltpu.VMEM((own, width + LANES), BF16),
            pltpu.VMEM((own, width), BF16),
            pltpu.VMEM((n_q, own, width + LANES), BF16),
            pltpu.VMEM((n_p, own, width), BF16),
            pltpu.VMEM((n_q * own, width + LANES), F32),
            pltpu.VMEM((n_p * own, width), F32),
            pltpu.VMEM((n_q, 1, 3 * LANES), F32),
            pltpu.VMEM((1, 3 * LANES), F32),
            pltpu.VMEM((n_p, own, width), BF16),
            pltpu.VMEM((PLANE, own, width), BF16),
            pltpu.VMEM((n_p, own, width), BF16),
            pltpu.VMEM((n_p * own, n_q * own), F32),
            pltpu.VMEM((n_p * own, n_q * own), F32),
            pltpu.VMEM((Z, own, width), BF16),
            pltpu.VMEM((Z, own, width), BF16),
            pltpu.VMEM((PLANE, 1, LANES), F32),
            pltpu.VMEM((1, LANES), F32),
            pltpu.SemaphoreType.DMA((7,)),
            pltpu.SemaphoreType.DMA((9,)),
            pltpu.SemaphoreType.DMA((9,)),
            pltpu.SemaphoreType.DMA((Z,)),
        ],
        compiler_params=pltpu.CompilerParams(
            collective_id=0, has_side_effects=True, vmem_limit_bytes=32 * 1024 * 1024),
    )(*(pltpu.with_memory_space_constraint(a, pltpu.HBM) for a in (queries, passages, positive)))
    loss, gq, gp = pl.pallas_call(
        hand_out,
        out_shape=(
            jax.ShapeDtypeStruct((1, LANES), F32),
            jax.ShapeDtypeStruct((own, width), BF16),
            jax.ShapeDtypeStruct((own, width), BF16),
        ),
        in_specs=[vmem],
        out_specs=(hbm, hbm, hbm),
        scratch_shapes=[pltpu.VMEM((2, own, width), BF16), pltpu.SemaphoreType.DMA((3,))],
    )(pltpu.with_memory_space_constraint(out, pltpu.VMEM))
    return loss[0, 0], gq, gp


def solution(mesh):
    placed = (P(("row", "col"), None), P(("row", "col"), None), P(("row", "col")))
    return jax.shard_map(
        per_device,
        mesh=mesh,
        in_specs=placed,
        out_specs=(P(), P(("row", "col"), None), P(("row", "col"), None)),
        check_vma=False,
    )
```

time: 31.4 us -> 30.1 us (0.959)
  Pallas kernels: 30.6 us -> 29.4 us
    pallas_call x1, Pallas kernels: 30 us -> 28.7 us  [per_device(): pl.pallas_call(functools.partial(kernel, n_q * own * PLANE), out_shape=ja...]
where the time goes in v5:
time: 30.1 us; the launch traced here: 30 us
  Pallas kernels  29.4 us (98%)
  between operations  0.64 us (2%)
    pallas_call x1, Pallas kernels, per_device(): pl.pallas_call(functools.partial(kernel, n_q * own * PLANE), out_shape=ja...  28.7 us
    pallas_call x1, Pallas kernels, per_device(): pl.pallas_call(hand_out, out_shape=(jax.ShapeDtypeStruct((1, LANES), F32)...  0.65 us

profile of v5, /device:TPU:1, one launch (start us, length us, event | category | flops | bytes accessed | tf_op | source)
XLA Modules:
  0.0 30.0 jit_solution(819918237335480950)
XLA Ops:
  0.6 28.7 %shard_map.58.all_ref = f32[3,4,2560]{2,1,0:T(4,128)S(1)} custom-call(bf16[4,2560]{1,0:T(4,128)(2,1)} %q_hbm.1, bf16[4,2560]{1,0:T(4,128)(2,1)} %p_hbm.1, s32[4]{0:T(128)} %pos_hbm.1), custom_call_target="tpu_custom_call" | custom-call | tf_op jit(solution)/shard_map/pallas_call | solution.py:255
  29.3 0.7 %shard_map.59 = (f32[1,128]{1,0:T(1,128)}, bf16[4,2560]{1,0:T(4,128)(2,1)}, bf16[4,2560]{1,0:T(4,128)(2,1)}) custom-call(f32[3,4,2560]{2,1,0:T(4,128)S(1)} %shard_map.58.all_ref), custom_call_target="tpu_custom_call" | custom-call | tf_op jit(solution)/shard_map/pallas_call | solution.py:287

commit v6 on v5

--- a/solution.py
+++ b/solution.py
@@ -180,10 +180,10 @@
     lossbuf[pl.ds(chip, 1)] = loss_own[...][None]
     for step in PLANE_STEPS:
         send(loss_own, lossbuf.at[chip], on_plane(step), 6).start()
-    for at in range(0, width, 256):
-        part = jnp.dot(weights, queries[:, at:at + 256], preferred_element_type=F32).astype(BF16)
+    for at in range(0, width, 512):
+        part = jnp.dot(weights, queries[:, at:at + 512], preferred_element_type=F32).astype(BF16)
         for s in range(p_count):
-            gp_send[s, :, at:at + 256] = part[s * own:(s + 1) * own]
+            gp_send[s, :, at:at + 512] = part[s * own:(s + 1) * own]
     for step in PLANE_STEPS:
         send(gp_send.at[x_slot[step[0]] + ys[step[1]]], gp_recv.at[chip], on_plane(step), 4).start()
     own_gp = pltpu.make_async_copy(gp_send.at[chip], gp_recv.at[chip], local_sem.at[5])
@@ -192,15 +192,14 @@
     def of_mine(w):
         return jnp.where(core == 0, w[:, :n_q // 2], w[:, n_q // 2:]).astype(BF16)
 
-    w_own, w_other = of_mine(wide), of_mine(weigh(score_other[...], matched_other))
-
-    def share(w, block):
-        return lax.dot_general(w, block, (((0,), (0,)), ((), ())), preferred_element_type=F32)
-
-    for at in range(0, width, 256):
-        part = (share(w_own, passages[:, at:at + 256]) + share(w_other, passages_other[:, at:at + 256])).astype(BF16)
+    w_mine = jnp.concatenate([of_mine(wide), of_mine(weigh(score_other[...], matched_other))], axis=0)
+    all_passages = jnp.concatenate([passages, passages_other], axis=0)
+
+    for at in range(0, width, 512):
+        part = lax.dot_general(w_mine, all_passages[:, at:at + 512], (((0,), (0,)), ((), ())),
+                               preferred_element_type=F32).astype(BF16)
         for s in range(Z):
-            gq_send[s, :, at:at + 256] = part[s * own:(s + 1) * own]
+            gq_send[s, :, at:at + 512] = part[s * own:(s + 1) * own]
     for step in LINE_STEPS:
         send(gq_send.at[zs[step]], gq_recv.at[z], on_line(step, core), 5).start()
     own_gq = pltpu.make_async_copy(gq_send.at[z], gq_recv.at[z], local_sem.at[6])
@@ -208,10 +207,7 @@
 
     wait_recv(lossbuf.at[pl.ds(0, PLANE - 1)], 6)
     loss = jnp.sum(jnp.sum(lossbuf[...], axis=0)) / total
-    at_first = (lax.broadcasted_iota(jnp.int32, (own, LANES), 0) == 0) & (lax.broadcasted_iota(jnp.int32, (own, LANES), 1) == 0)
-    g_ref[2] = jnp.zeros(g_ref.shape[1:], F32)
-    g_ref[2, :, :LANES] = jnp.where(at_first, loss, 0.0)
-
+    g_ref[2, :, :LANES] = jnp.broadcast_to(loss, (own, LANES))
     own_gp.wait()
     wait_recv(gp_send.at[pl.ds(0, p_count - 1)], 4)
     for h in range(2):

time: 30.1 us -> 30.1 us (level)
  no operation moved by 1% of the time
where the time goes in v6:
time: 30.1 us; the launch traced here: 30 us
  Pallas kernels  29.3 us (97%)
  between operations  0.64 us (2%)
    pallas_call x1, Pallas kernels, per_device(): pl.pallas_call(functools.partial(kernel, n_q * own * PLANE), out_shape=ja...  28.7 us
    pallas_call x1, Pallas kernels, per_device(): pl.pallas_call(hand_out, out_shape=(jax.ShapeDtypeStruct((1, LANES), F32)...  0.65 us

profile of v6, /device:TPU:1, one launch (start us, length us, event | category | flops | bytes accessed | tf_op | source)
XLA Modules:
  0.0 30.0 jit_solution(16187970399409904279)
XLA Ops:
  0.6 28.7 %shard_map.58.all_ref = f32[3,4,2560]{2,1,0:T(4,128)S(1)} custom-call(bf16[4,2560]{1,0:T(4,128)(2,1)} %q_hbm.1, bf16[4,2560]{1,0:T(4,128)(2,1)} %p_hbm.1, s32[4]{0:T(128)} %pos_hbm.1), custom_call_target="tpu_custom_call" | custom-call | tf_op jit(solution)/shard_map/pallas_call | solution.py:251
  29.3 0.7 %shard_map.59 = (f32[1,128]{1,0:T(1,128)}, bf16[4,2560]{1,0:T(4,128)(2,1)}, bf16[4,2560]{1,0:T(4,128)(2,1)}) custom-call(f32[3,4,2560]{2,1,0:T(4,128)S(1)} %shard_map.58.all_ref), custom_call_target="tpu_custom_call" | custom-call | tf_op jit(solution)/shard_map/pallas_call | solution.py:283
